TPU v7x, 32 devices: a whole 2x2x4 slice. The times are simulated.
32 devices in a mesh: dp: 16 (over z, x, core), fsdp: 2 (over y).
Axes of the slice: x: 2, y: 2, z: 4, core: 2. Of those that a mesh axis runs over, the one named last changes fastest.
Arguments:
- tokens: bfloat16 [32, 561, 768], P(('dp', 'fsdp')), may hold values from -6 to 6
- coords: int32 [32, 2, 561], P(('dp', 'fsdp')), may hold values from 0 to 1023
- rel_pos: int32 [32, 561, 561], P(('dp', 'fsdp')), may hold values from 0 to 31
- rel_box: int32 [32, 2, 561, 561], P(('dp', 'fsdp')), may hold values from 0 to 63
- entity_pairs: int32 [32, 128, 2], P(('dp', 'fsdp')), may hold values from -1 to 560, as said below
- entity_grad: bfloat16 [32, 128, 2, 768], P(('dp', 'fsdp')), may hold values from -6 to 6
- w_qkv: bfloat16 [768, 2304], P(('dp', 'fsdp')), may hold values from -0.21875 to 0.21875
- w_attn_out: bfloat16 [768, 768], P(('dp', 'fsdp')), may hold values from -1.75 to 1.75
- dcpe_table: bfloat16 [2048, 768], P(('dp', 'fsdp')), may hold values from -3 to 3
- biases: bfloat16 [6, 768], P(None, ('dp', 'fsdp')), may hold values from -1.796875 to 1.796875
- norm_gains: bfloat16 [2, 768], P(None, ('dp', 'fsdp')), may hold values from 0.5 to 1.5
- w_ff_in: bfloat16 [768, 3072], P(('dp', 'fsdp')), may hold values from -0.21875 to 0.21875
- w_ff_out: bfloat16 [3072, 768], P(('dp', 'fsdp')), may hold values from -0.109375 to 0.109375
- ff_bias: bfloat16 [3072], P(('dp', 'fsdp')), may hold values from -1.796875 to 1.796875
- rel_table: bfloat16 [160, 12], replicated, may hold values from -3 to 3
Outputs:
- layer_out: bfloat16 [32, 561, 768], P(('dp', 'fsdp'))
- input_grad: float32 [32, 561, 768], P(('dp', 'fsdp'))
- w_qkv_grad: float32 [768, 2304], P(('dp', 'fsdp'))
- w_attn_out_grad: float32 [768, 768], P(('dp', 'fsdp'))
- dcpe_table_grad: float32 [2048, 768], P(('dp', 'fsdp'))
- biases_grad: float32 [6, 768], P(None, ('dp', 'fsdp'))
- norm_gains_grad: float32 [2, 768], P(None, ('dp', 'fsdp'))
- w_ff_in_grad: float32 [768, 3072], P(('dp', 'fsdp'))
- w_ff_out_grad: float32 [3072, 768], P(('dp', 'fsdp'))
- ff_bias_grad: float32 [3072], P(('dp', 'fsdp'))
- rel_table_grad: float32 [160, 12], replicated
Inputs may be any that keep to these rules, and one draw needn't show every extreme that they name: `entity_pairs`: each entry names a token of its page or is -1; a live pair names two different tokens, a padded pair is -1 twice, and a page's padded pairs follow its live ones. A token may be named by several slots of its page.
All inputs are finite; a program needn't handle non-finite values.
Results may differ from a plain program's by a relative error of at most 0.015.
The roundings to bfloat16 on the way count: a program that leaves them out, or rounds other values in their place, can miss the bound.
Values may be sent and summed in bfloat16 or wider, within the bound.
No kernel may reach another device: no remote copies, remote signals or barrier semaphores. Data moves between devices by JAX's collectives and lax.ppermute only.
A program may use at most 256 MiB of HBM per device.

v0:
```python
from functools import partial

import jax
import jax.numpy as jnp
from jax import lax
from jax.sharding import PartitionSpec as P

HEADS = 12
HEAD_DIM = 64
B1 = 32
B2 = 64
PAGE = 561


epsilon = 1e-05


def norm_rows(values, gain, shift):
    row_mean = jnp.mean(values, axis=-1, keepdims=True)
    centred = values - row_mean
    variance = jnp.mean(centred * centred, axis=-1, keepdims=True)
    return centred * lax.rsqrt(variance + epsilon) * gain + shift


def gelu_exact(values):
    return jax.nn.gelu(values, approximate=False)


def to_heads(values, page_count):
    return values.reshape(page_count, PAGE, HEADS, HEAD_DIM).transpose(0, 2, 1, 3)


def from_heads(values):
    return values.transpose(0, 2, 1, 3).reshape(-1, HEADS * HEAD_DIM)


def bucket_hots(pos_part, box_part):
    first = (pos_part[..., None] == lax.iota(jnp.int32, B1)).astype(jnp.bfloat16)
    across = (box_part[0][..., None] == lax.iota(jnp.int32, B2)).astype(jnp.bfloat16)
    downward = (box_part[1][..., None] == lax.iota(jnp.int32, B2)).astype(jnp.bfloat16)
    return (first, across, downward)


def split_thirds(rel_pos, rel_box):
    third_rows = rel_pos.shape[0] // 3
    pos_parts = rel_pos.reshape(3, third_rows, rel_pos.shape[1])
    box_parts = rel_box.reshape(2, 3, third_rows, rel_box.shape[2]).transpose(1, 0, 2, 3)
    return (pos_parts, box_parts)


def page_bias(bias_table, rel_pos, rel_box):
    pos_parts, box_parts = split_thirds(rel_pos, rel_box)

    def page_one_third(pieces):
        first, across, downward = bucket_hots(pieces[0], pieces[1])
        partial_bias = jnp.einsum(
            "qkb,bh->hqk", first, bias_table[:B1], preferred_element_type=jnp.float32
        )
        partial_bias = partial_bias + jnp.einsum(
            "qkb,bh->hqk", across, bias_table[B1 : B1 + B2], preferred_element_type=jnp.float32
        )
        return partial_bias + jnp.einsum(
            "qkb,bh->hqk", downward, bias_table[B1 + B2 :], preferred_element_type=jnp.float32
        )

    blocks = lax.map(page_one_third, (pos_parts, box_parts))
    return blocks.transpose(1, 0, 2, 3).reshape(
        bias_table.shape[1], rel_pos.shape[0], rel_pos.shape[1]
    )


def table_grad(d_scores, rel_pos, rel_box):
    pos_parts, box_parts = split_thirds(rel_pos, rel_box)
    head_count = d_scores.shape[0]
    score_parts = d_scores.reshape(head_count, 3, pos_parts.shape[1], d_scores.shape[2]).transpose(
        1, 0, 2, 3
    )

    def table_one_third(running, pieces):
        first, across, downward = bucket_hots(pieces[0], pieces[1])
        portion = pieces[2]
        gathered = jnp.concatenate(
            [
                jnp.einsum("qkb,hqk->bh", first, portion, preferred_element_type=jnp.float32),
                jnp.einsum("qkb,hqk->bh", across, portion, preferred_element_type=jnp.float32),
                jnp.einsum("qkb,hqk->bh", downward, portion, preferred_element_type=jnp.float32),
            ],
            axis=0,
        )
        return (running + gathered, None)

    initial = jnp.zeros((B1 + 2 * B2, head_count), jnp.float32)
    running, _ = lax.scan(table_one_third, initial, (pos_parts, box_parts, score_parts))
    return running


def page_forward(bias_table, inputs):
    query_page, key_page, value_page, pos_page, box_page = inputs
    scores = jnp.einsum(
        "hqd,hkd->hqk", query_page, key_page, preferred_element_type=jnp.float32
    ) + page_bias(bias_table, pos_page, box_page)
    largest = jnp.max(scores, axis=-1, keepdims=True)
    raised = jnp.exp(scores - largest)
    row_total = jnp.sum(raised, axis=-1, keepdims=True)
    attention = (raised / row_total).astype(jnp.bfloat16)
    context = jnp.einsum("hqk,hkd->hqd", attention, value_page, preferred_element_type=jnp.float32)
    return (context, (largest + jnp.log(row_total))[..., 0])


def page_backward(bias_table, inputs):
    query_page, key_page, value_page, log_total, d_context, pos_page, box_page = inputs
    scores = jnp.einsum(
        "hqd,hkd->hqk", query_page, key_page, preferred_element_type=jnp.float32
    ) + page_bias(bias_table, pos_page, box_page)
    attention = jnp.exp(scores - log_total[..., None])
    d_attention = jnp.einsum(
        "hqd,hkd->hqk", d_context, value_page, preferred_element_type=jnp.float32
    )
    centre = jnp.sum(attention * d_attention, axis=-1, keepdims=True)
    d_scores = (attention * (d_attention - centre)).astype(jnp.bfloat16)
    d_query = (
        jnp.einsum("hqk,hkd->hqd", d_scores, key_page, preferred_element_type=jnp.float32).astype(
            jnp.bfloat16
        )
        * 0.125
    )
    d_key = jnp.einsum(
        "hqk,hqd->hkd", d_scores, query_page, preferred_element_type=jnp.float32
    ).astype(jnp.bfloat16)
    d_value = jnp.einsum(
        "hqk,hqd->hkd",
        attention.astype(jnp.bfloat16),
        d_context,
        preferred_element_type=jnp.float32,
    ).astype(jnp.bfloat16)
    return (d_query, d_key, d_value, table_grad(d_scores, pos_page, box_page))


def forward_local(attn_full, ff_full, bias_table, tokens, coords, rel_pos, rel_box):
    w_qkv, w_attn_out, dcpe_table, biases, norm_gains = attn_full
    w_ff_in, w_ff_out, ff_bias = ff_full
    page_count = tokens.shape[0]
    model_width = tokens.shape[2]
    hot_width = dcpe_table.shape[0]
    columns = lax.iota(jnp.int32, hot_width)
    position_hot = (
        ((coords[:, 0, :, None] == columns) | (coords[:, 1, :, None] + hot_width // 2 == columns))
        .astype(jnp.bfloat16)
        .reshape(-1, hot_width)
    )
    begin = tokens.reshape(-1, model_width).astype(jnp.float32) + jnp.dot(
        position_hot, dcpe_table, preferred_element_type=jnp.float32
    )
    begin_rows = begin.astype(jnp.bfloat16)
    united_proj = jnp.dot(begin_rows, w_qkv, preferred_element_type=jnp.float32)
    shifts = biases.astype(jnp.float32)
    scales = norm_gains.astype(jnp.float32)
    query_heads = to_heads(
        ((united_proj[:, :model_width] + shifts[0]) * 0.125).astype(jnp.bfloat16), page_count
    )
    key_heads = to_heads(
        united_proj[:, model_width : 2 * model_width].astype(jnp.bfloat16), page_count
    )
    value_heads = to_heads(
        (united_proj[:, 2 * model_width :] + shifts[1]).astype(jnp.bfloat16), page_count
    )
    context_heads, log_total = lax.map(
        partial(page_forward, bias_table), (query_heads, key_heads, value_heads, rel_pos, rel_box)
    )
    context = from_heads(context_heads).astype(jnp.bfloat16)
    attended = jnp.dot(context, w_attn_out, preferred_element_type=jnp.float32) + shifts[2]
    mid_norm = norm_rows(begin + attended, scales[0], shifts[3])
    mid_rows = mid_norm.astype(jnp.bfloat16)
    ff_inner = jnp.dot(mid_rows, w_ff_in, preferred_element_type=jnp.float32) + ff_bias.astype(
        jnp.float32
    )
    ff_act = gelu_exact(ff_inner).astype(jnp.bfloat16)
    ff_outer = jnp.dot(ff_act, w_ff_out, preferred_element_type=jnp.float32) + shifts[4]
    result = norm_rows(mid_norm + ff_outer, scales[1], shifts[5])
    return (
        position_hot,
        begin,
        begin_rows,
        query_heads,
        key_heads,
        value_heads,
        log_total,
        context,
        attended,
        mid_norm,
        mid_rows,
        ff_inner,
        ff_act,
        ff_outer,
        result,
    )


def on_device(
    tokens,
    coords,
    rel_pos,
    rel_box,
    entity_pairs,
    entity_grad,
    w_qkv,
    w_attn_out,
    dcpe_table,
    biases,
    norm_gains,
    w_ff_in,
    w_ff_out,
    ff_bias,
    rel_table,
):
    page_count = tokens.shape[0]
    model_width = tokens.shape[2]
    attn_full = (
        lax.all_gather(w_qkv, ("dp", "fsdp"), axis=0, tiled=True),
        lax.all_gather(w_attn_out, ("dp", "fsdp"), axis=0, tiled=True),
        lax.all_gather(dcpe_table, ("dp", "fsdp"), axis=0, tiled=True),
        lax.all_gather(biases, ("dp", "fsdp"), axis=1, tiled=True),
        lax.all_gather(norm_gains, ("dp", "fsdp"), axis=1, tiled=True),
    )
    ff_full = (
        lax.all_gather(w_ff_in, ("dp", "fsdp"), axis=0, tiled=True),
        lax.all_gather(w_ff_out, ("dp", "fsdp"), axis=0, tiled=True),
        lax.all_gather(ff_bias, ("dp", "fsdp"), axis=0, tiled=True),
    )
    stored = forward_local(attn_full, ff_full, rel_table, tokens, coords, rel_pos, rel_box)
    layer_out = stored[14].astype(jnp.bfloat16).reshape(tokens.shape)
    attn_full = (
        lax.all_gather(w_qkv, ("dp", "fsdp"), axis=0, tiled=True),
        lax.all_gather(w_attn_out, ("dp", "fsdp"), axis=0, tiled=True),
        lax.all_gather(dcpe_table, ("dp", "fsdp"), axis=0, tiled=True),
        lax.all_gather(biases, ("dp", "fsdp"), axis=1, tiled=True),
        lax.all_gather(norm_gains, ("dp", "fsdp"), axis=1, tiled=True),
    )
    ff_full = (
        lax.all_gather(w_ff_in, ("dp", "fsdp"), axis=0, tiled=True),
        lax.all_gather(w_ff_out, ("dp", "fsdp"), axis=0, tiled=True),
        lax.all_gather(ff_bias, ("dp", "fsdp"), axis=0, tiled=True),
    )
    stored = forward_local(attn_full, ff_full, rel_table, tokens, coords, rel_pos, rel_box)
    (
        position_hot,
        begin,
        begin_rows,
        query_heads,
        key_heads,
        value_heads,
        log_total,
        context,
        attended,
        mid_norm,
        mid_rows,
        ff_inner,
        ff_act,
        ff_outer,
        result,
    ) = stored
    full_qkv, full_attn_out, full_dcpe, full_biases, full_gains = attn_full
    full_ff_in, full_ff_out, full_ff_bias = ff_full
    shifts = full_biases.astype(jnp.float32)
    scales = full_gains.astype(jnp.float32)
    slot_ids = lax.iota(jnp.int32, PAGE)
    pair_hot = (entity_pairs.reshape(page_count, -1)[:, :, None] == slot_ids).astype(jnp.bfloat16)
    out_cot = jnp.einsum(
        "gsp,gsd->gpd",
        pair_hot,
        entity_grad.reshape(page_count, pair_hot.shape[1], model_width),
        preferred_element_type=jnp.float32,
    ).reshape(-1, model_width)
    _, second_pull = jax.vjp(norm_rows, mid_norm + ff_outer, scales[1], shifts[5])
    d_sum, gain_two, shift_two = second_pull(out_cot)
    d_outer = d_sum.astype(jnp.bfloat16)
    grad_ff_out = jnp.einsum("rf,rd->fd", ff_act, d_outer, preferred_element_type=jnp.float32)
    d_act = jnp.einsum("rd,fd->rf", d_outer, full_ff_out, preferred_element_type=jnp.float32)
    _, gelu_pull = jax.vjp(gelu_exact, ff_inner)
    d_inner = gelu_pull(d_act)[0].astype(jnp.bfloat16)
    grad_ff_in = jnp.einsum("rd,rf->df", mid_rows, d_inner, preferred_element_type=jnp.float32)
    grad_ff_bias = jnp.sum(d_inner, axis=0, dtype=jnp.float32)
    d_mid = d_sum + jnp.einsum("rf,df->rd", d_inner, full_ff_in, preferred_element_type=jnp.float32)
    ff_owned = (
        lax.psum_scatter(grad_ff_in, ("dp", "fsdp"), scatter_dimension=0, tiled=True),
        lax.psum_scatter(grad_ff_out, ("dp", "fsdp"), scatter_dimension=0, tiled=True),
        lax.psum_scatter(grad_ff_bias, ("dp", "fsdp"), scatter_dimension=0, tiled=True),
    )
    _, first_pull = jax.vjp(norm_rows, begin + attended, scales[0], shifts[3])
    d_pre, gain_one, shift_one = first_pull(d_mid)
    d_att = d_pre.astype(jnp.bfloat16)
    grad_attn_out = jnp.einsum("rd,re->de", context, d_att, preferred_element_type=jnp.float32)
    d_context = jnp.einsum(
        "re,de->rd", d_att, full_attn_out, preferred_element_type=jnp.float32
    ).astype(jnp.bfloat16)
    d_query, d_key, d_value, table_parts = lax.map(
        partial(page_backward, rel_table),
        (
            query_heads,
            key_heads,
            value_heads,
            log_total,
            to_heads(d_context, page_count),
            rel_pos,
            rel_box,
        ),
    )
    d_united = jnp.concatenate(
        [from_heads(d_query), from_heads(d_key), from_heads(d_value)], axis=1
    )
    grad_qkv = jnp.einsum("rd,re->de", begin_rows, d_united, preferred_element_type=jnp.float32)
    input_grad = d_pre + jnp.einsum(
        "re,de->rd", d_united, full_qkv, preferred_element_type=jnp.float32
    )
    grad_dcpe = jnp.einsum(
        "rc,rd->cd",
        position_hot,
        input_grad.astype(jnp.bfloat16),
        preferred_element_type=jnp.float32,
    )
    grad_biases = jnp.stack(
        [
            jnp.sum(d_united[:, :model_width], axis=0, dtype=jnp.float32),
            jnp.sum(d_united[:, 2 * model_width :], axis=0, dtype=jnp.float32),
            jnp.sum(d_att, axis=0, dtype=jnp.float32),
            shift_one,
            jnp.sum(d_outer, axis=0, dtype=jnp.float32),
            shift_two,
        ]
    )
    grad_gains = jnp.stack([gain_one, gain_two])
    table_summed = lax.psum(jnp.sum(table_parts, axis=0), ("dp", "fsdp"))
    input_grad = input_grad.reshape(tokens.shape)
    attn_owned = (
        lax.psum_scatter(grad_qkv, ("dp", "fsdp"), scatter_dimension=0, tiled=True),
        lax.psum_scatter(grad_attn_out, ("dp", "fsdp"), scatter_dimension=0, tiled=True),
        lax.psum_scatter(grad_dcpe, ("dp", "fsdp"), scatter_dimension=0, tiled=True),
        lax.psum_scatter(grad_biases, ("dp", "fsdp"), scatter_dimension=1, tiled=True),
        lax.psum_scatter(grad_gains, ("dp", "fsdp"), scatter_dimension=1, tiled=True),
    )
    return (
        layer_out,
        input_grad,
        attn_owned[0],
        attn_owned[1],
        attn_owned[2],
        attn_owned[3],
        attn_owned[4],
        ff_owned[0],
        ff_owned[1],
        ff_owned[2],
        table_summed,
    )


def solution(mesh):
    return jax.shard_map(
        on_device,
        mesh=mesh,
        in_specs=(
            P(("dp", "fsdp"), None, None),
            P(("dp", "fsdp"), None, None),
            P(("dp", "fsdp"), None, None),
            P(("dp", "fsdp"), None, None, None),
            P(("dp", "fsdp"), None, None),
            P(("dp", "fsdp"), None, None, None),
            P(("dp", "fsdp"), None),
            P(("dp", "fsdp"), None),
            P(("dp", "fsdp"), None),
            P(None, ("dp", "fsdp")),
            P(None, ("dp", "fsdp")),
            P(("dp", "fsdp"), None),
            P(("dp", "fsdp"), None),
            P(("dp", "fsdp")),
            P(),
        ),
        out_specs=(
            P(("dp", "fsdp"), None, None),
            P(("dp", "fsdp"), None, None),
            P(("dp", "fsdp"), None),
            P(("dp", "fsdp"), None),
            P(("dp", "fsdp"), None),
            P(None, ("dp", "fsdp")),
            P(None, ("dp", "fsdp")),
            P(("dp", "fsdp"), None),
            P(("dp", "fsdp"), None),
            P(("dp", "fsdp")),
            P(),
        ),
        check_vma=False,
    )
```

profile of v0, /device:TPU:0, one launch (start us, length us, event | category | flops | bytes accessed | tf_op | source)
XLA Modules:
  0.0 1022.8 jit_solution(5345740920127555831)
XLA Ops:
  11.4 70.6 %all-gather = bf16[32,24,6]{1,2,0:T(8,128)(2,1)S(1)} all-gather(bf16[1,24,6]{1,2,0:T(8,128)(2,1)} %bitcast.202), channel_id=1, replica_groups=mesh['dp'=16,'fsdp'=2] {'dp','fsdp'}, dimensions={0}, use_global_device_ids=true | all-gather | bytes 9504 | tf_op jit(solution)/shard_map/all_gather | solution.py:222
  93.6 71.5 %while.41 = (s32[]{:T(128)}, f32[3,12,187,561]{3,1,2,0:T(8,128)}, s32[3,187,561]{2,1,0:T(8,128)}, bf16[160,12]{0,1:T(8,128)(2,1)S(1)}, s32[3,2,187,561]{3,2,1,0:T(8,128)S(1)}, /*index=5*/s32[]{:T(128)}, s32[]{:T(128)}, s32[]{}) while((s32[]{:T(128)}, f32[3,12,187,561]{3,1,2,0:T(8,128)}, s32[3,187,561]{2,1,0:T(8,128)}, ...), condition=%wide.region_1.2_spmd, body=%wide.region_0.1_spmd.sunk | while | flops 422145760 | bytes 37054868 | solution.py:66
  99.5 7.6 fusion.139
  108.1 9.4 bitcast_dynamic-update-slice_fusion.2
  123.2 7.6 fusion.139
  131.8 9.6 bitcast_dynamic-update-slice_fusion.2
  147.1 7.6 fusion.139
  155.7 9.4 bitcast_dynamic-update-slice_fusion.2
  165.1 63.0 %all-gather.1 = bf16[32,24,2]{1,2,0:T(2,128)(2,1)S(1)} all-gather(bf16[1,24,2]{1,2,0:T(2,128)(2,1)S(1)} %bitcast.203), channel_id=1, replica_groups=mesh['dp'=16,'fsdp'=2] {'dp','fsdp'}, dimensions={0}, use_global_device_ids=true | all-gather | bytes 3168 | tf_op jit(solution)/shard_map/all_gather | solution.py:223
  228.7 38.5 %all-reduce = bf16[3072]{0:T(1024)(128)(2,1)S(1)} all-reduce(bf16[3072]{0:T(1024)(128)(2,1)S(1)} %dynamic-update-slice), channel_id=1, replica_groups=mesh['dp'=16,'fsdp'=2] {'dp','fsdp'}, use_global_device_ids=true, to_apply=%add | all-reduce | flops 3072 | bytes 12288
  286.4 21.0 %fusion.89 = (f32[12,561]{1,0:T(8,128)S(1)}, f32[12,561,561]{2,1,0:T(8,128)}) fusion(f32[12,561,561]{2,0,1:T(8,128)} %bitcast.184, bf16[12,561,64]{1,2,0:T(8,128)(2,1)S(1)} %bitcast.185, bf16[12,561,64]{1,2,0:T(8,128)(2,1)S(1)} %bitcast.190), kind=kOutput, calls=%fused_computation.158 | convolution fusion | flops 490958016 | bytes 31963536 | tf_op jit(solution)/shard_map/while/body/eval_jaxpr/hqd,hkd->hqk/dot_general | solution.py:99
  307.4 9.4 fusion.36
  328.5 22.1 %multiply_convert_fusion.1 = (bf16[561,3072]{1,0:T(8,128)(2,1)}, f32[561,3072]{1,0:T(8,128)}, f32[561,3072]{1,0:T(8,128)}) fusion(f32[3072]{0:T(1024)S(1)} %convert_element_type.144, bf16[768,3072]{1,0:T(8,128)(2,1)} %all-gather.14.cloned.1.call-done, f32[561,768]{1,0:T(8,128)S(1)} %get-tuple-element.331, f32[768]{0:T(1024)S(1)} %get-tuple-element.277, ...), kind=kOutput, calls=%fused_computation.59 | convolution fusion | flops 2763028224 | bytes 23698824 | tf_op jit(solution)/shard_map/dot_general | solution.py:174
  361.0 9.4 convert_reduce_fusion
  385.6 12.6 %multiply_reduce_fusion = (f32[12,561]{1,0:T(8,128)S(1)}, f32[12,561,561]{2,1,0:T(8,128)}) fusion(f32[12,561,561]{2,1,0:T(8,128)} %get-tuple-element.329, f32[12,561]{1,0:T(8,128)S(1)} %log_add_fusion, bf16[12,561,64]{1,2,0:T(8,128)(2,1)} %bitcast.188, bf16[12,561,64]{1,2,0:T(8,128)(2,1)} %bitcast.192), kind=kOutput, calls=%fused_computation.46 | convolution fusion | flops 494734656 | bytes 31990464 | tf_op jit(solution)/shard_map/while/body/eval_jaxpr/hqd,hkd->hqk/dot_general | solution.py:116
  398.2 12.6 %multiply_convert_fusion = bf16[12,561,561]{2,1,0:T(8,128)(2,1)S(1)} fusion(f32[12,561,561]{2,1,0:T(8,128)} %get-tuple-element.338, f32[12,561,561]{2,1,0:T(8,128)} %get-tuple-element.329, f32[12,561]{1,0:T(8,128)S(1)} %get-tuple-element.337, f32[12,561]{1,0:T(8,128)S(1)} %log_add_fusion), kind=kLoop, calls=%fused_computation.45 | loop fusion | flops 15106608 | bytes 37820376 | tf_op jit(solution)/shard_map/while/body/eval_jaxpr/convert_element_type | solution.py:120
  418.2 8.6 convert_reduce_fusion.1
  438.7 8.2 fusion.68
  447.0 9.7 fusion.93
  456.8 8.6 fusion.82
  465.5 10.6 %copy.77 = bf16[12,561,561]{2,0,1:T(8,128)(2,1)} copy(bf16[12,561,561]{2,1,0:T(8,128)(2,1)} %copy-done.1) | data formatting | bytes 15106608 | tf_op jit(solution)/shard_map/while/body/eval_jaxpr/reshape | solution.py:75
  479.3 62.9 %while.42 = (s32[]{:T(128)}, f32[160,12]{0,1:T(8,128)S(1)}, s32[3,187,561]{2,1,0:T(8,128)}, bf16[3,12,187,561]{3,1,2,0:T(8,128)(2,1)}, s32[3,2,187,561]{3,2,1,0:T(8,128)}, /*index=5*/s32[]{:T(128)}, s32[]{:T(128)}, s32[]{}) while((s32[]{:T(128)}, f32[160,12]{0,1:T(8,128)S(1)}, s32[3,187,561]{2,1,0:T(8,128)}, ...), condition=%wide.region_31.32_spmd.clone, body=%wide.region_30.31_spmd.clone.sunk | while | flops 419635680 | bytes 15298307 | solution.py:93
  480.8 6.9 fusion.143
  501.6 7.0 fusion.143
  508.5 7.0 fusion.144
  522.6 7.0 fusion.143
  529.6 7.0 fusion.144
  542.2 45.1 %all-reduce.4 = (f32[6,768]{1,0:T(8,128)S(1)}, f32[2,768]{1,0:T(2,128)S(1)}, f32[3072]{0:T(1024)S(1)}, f32[160,12]{0,1:T(8,128)}) all-reduce(f32[6,768]{1,0:T(8,128)S(1)} %stack.26, f32[2,768]{1,0:T(2,128)S(1)} %pad_maximum_fusion.3, f32[3072]{0:T(1024)S(1)} %get-tuple-element.309, ...), channel_id=5, replica_groups=mesh['dp'=16,'fsdp'=2] {'dp','fsdp'}, use_global_device_ids=true, to_apply=%region_22.23.clone | all-reduce | flops 11136 | bytes 89088
  589.2 18.4 %reduce-scatter.12.cloned.1.call-done = f32[64,768]{1,0:T(8,128)} async-done(((f32[2048,768]{1,0:T(8,128)}), f32[64,768]{1,0:T(8,128)}) %reduce-scatter.12.cloned.1.call-update) | async-done | bytes 196624 | tf_op jit(solution)/shard_map/reduce_scatter | solution.py:337
  607.6 124.7 %reduce-scatter.8.cloned.1.call-done = f32[24,2304]{1,0:T(8,128)} async-done(((f32[768,2304]{1,0:T(8,128)}), f32[24,2304]{1,0:T(8,128)}) %reduce-scatter.8.cloned.1.call-update) | async-done | bytes 221200 | tf_op jit(solution)/shard_map/reduce_scatter | solution.py:335
  732.3 142.5 %reduce-scatter.16.cloned.1.call-done = f32[96,768]{1,0:T(8,128)} async-done(((f32[3072,768]{1,0:T(8,128)}), f32[96,768]{1,0:T(8,128)}) %reduce-scatter.16.cloned.1.call-update) | async-done | bytes 294928 | tf_op jit(solution)/shard_map/reduce_scatter | solution.py:286
  874.8 141.0 %reduce-scatter.14.cloned.1.call-done = f32[24,3072]{1,0:T(8,128)} async-done(((f32[768,3072]{1,0:T(8,128)}), f32[24,3072]{1,0:T(8,128)}) %reduce-scatter.14.cloned.1.call-update) | async-done | bytes 294928 | tf_op jit(solution)/shard_map/reduce_scatter | solution.py:285
  (175 shorter events, 145.1 us)
Async XLA Ops:
  7.2 261.3 %all-gather.8.cloned.1.call-start = ((), (), s32[]{:S(2)}) async-start(), calls=%async_computation.5 | async-start | bytes 3244032 | tf_op jit(solution)/shard_map/all_gather | solution.py:221
  7.9 266.4 %all-gather.10.cloned.1.call-start = ((), (), s32[]{:S(2)}) async-start(), calls=%async_computation.6 | async-start | bytes 3649536 | tf_op jit(solution)/shard_map/all_gather | solution.py:219
  8.7 316.3 %all-gather.12.cloned.1.call-start = ((), (), s32[]{:S(2)}) async-start(), calls=%async_computation.7 | async-start | bytes 1216512 | tf_op jit(solution)/shard_map/all_gather | solution.py:220
  9.4 319.1 %all-gather.14.cloned.1.call-start = ((), (), s32[]{:S(2)}) async-start(), calls=%async_computation.8 | async-start | bytes 4866048 | tf_op jit(solution)/shard_map/all_gather | solution.py:226
  10.0 340.6 %all-gather.16.cloned.1.call-start = ((), (), s32[]{:S(2)}) async-start(), calls=%async_computation.9 | async-start | bytes 4866048 | tf_op jit(solution)/shard_map/all_gather | solution.py:227
  10.6 578.7 %reduce-scatter.10.cloned.1.call-start = ((), (), s32[]{:S(2)}) async-start(), calls=%async_computation.11 | async-start | bytes 2433024 | tf_op jit(solution)/shard_map/reduce_scatter | solution.py:336
  11.4 257.0 %copy-start.17 = (s32[561]{0:T(1024)}, s32[561]{0:T(1024)S(1)}, u32[]{:S(2)}) copy-start(s32[561]{0:T(1024)S(1)} %get-tuple-element.283) | copy-start | bytes 6736
  11.4 257.0 %copy-start.19 = (s32[561]{0:T(1024)}, s32[561]{0:T(1024)S(1)}, u32[]{:S(2)}) copy-start(s32[561]{0:T(1024)S(1)} %get-tuple-element.284) | copy-start | bytes 6736
  83.0 10.6 %copy-start.11 = (bf16[160,12]{0,1:T(8,128)(2,1)S(1)}, bf16[160,12]{0,1:T(8,128)(2,1)}, u32[]{:S(2)}) copy-start(bf16[160,12]{0,1:T(8,128)(2,1)} %param.33) | copy-start | bytes 11524
  93.6 71.5 %copy-start.23 = (bf16[2,24]{1,0:T(2,128)(2,1)S(1)}, bf16[2,24]{1,0:T(2,128)(2,1)}, u32[]{:S(2)}) copy-start(bf16[2,24]{1,0:T(2,128)(2,1)} %param.29) | copy-start | bytes 292
  93.6 134.8 %copy-start.25 = (bf16[96]{0:T(256)(128)(2,1)S(1)}, bf16[96]{0:T(256)(128)(2,1)}, u32[]{:S(2)}) copy-start(bf16[96]{0:T(256)(128)(2,1)} %param.32) | copy-start | bytes 580
  93.6 173.6 %copy-start.12 = (bf16[1,128,2,768]{3,2,1,0:T(2,128)(2,1)S(1)}, bf16[1,128,2,768]{3,2,1,0:T(2,128)(2,1)}, u32[]{:S(2)}) copy-start(bf16[1,128,2,768]{3,2,1,0:T(2,128)(2,1)} %param.24) | copy-start | bytes 1179652
  93.6 174.5 %copy-start.22 = (s32[1,128,2]{1,2,0:T(2,128)S(1)}, s32[1,128,2]{1,2,0:T(2,128)}, u32[]{:S(2)}) copy-start(s32[1,128,2]{1,2,0:T(2,128)} %param.23) | copy-start | bytes 3076
  165.1 109.2 %copy-start.2 = (s32[3,2,187,561]{3,2,1,0:T(8,128)}, s32[3,2,187,561]{3,2,1,0:T(8,128)S(1)}, u32[]{:S(2)}) copy-start(s32[3,2,187,561]{3,2,1,0:T(8,128)S(1)} %get-tuple-element.471) | copy-start | bytes 7553308
  283.4 23.9 %copy-start.4 = (bf16[561,768]{0,1:T(8,128)(2,1)}, bf16[561,768]{0,1:T(8,128)(2,1)S(1)}, u32[]{:S(2)}) copy-start(bf16[561,768]{0,1:T(8,128)(2,1)S(1)} %copy.62) | copy-start | bytes 2585092
  286.4 30.4 %copy-start.7 = (bf16[561,768]{0,1:T(8,128)(2,1)S(1)}, bf16[561,768]{0,1:T(8,128)(2,1)}, u32[]{:S(2)}) copy-start(bf16[561,768]{0,1:T(8,128)(2,1)} %copy.66) | copy-start | bytes 2585092
  307.4 11.3 %copy-start = (f32[12,561,561]{2,1,0:T(8,128)S(1)}, f32[12,561,561]{2,1,0:T(8,128)}, u32[]{:S(2)}) copy-start(f32[12,561,561]{2,1,0:T(8,128)} %get-tuple-element.329) | copy-start | bytes 45319828
  328.5 22.1 %copy-start.21 = (f32[768]{0:T(1024)S(1)}, f32[768]{0:T(1024)}, u32[]{:S(2)}) copy-start(f32[768]{0:T(1024)} %get-tuple-element.276) | copy-start | bytes 9220
  350.6 6.9 copy-start.13
  358.3 12.0 %slice-start = ((s8[4718592]{0:T(1024)(128)(4,1)}), s8[4194304]{0:T(1024)(128)(4,1)S(1)}, s32[]{:S(2)}) async-start(s8[4718592]{0:T(1024)(128)(4,1)} %bitcast.204), calls=%async_computation.15 | async-start | bytes 8388608
  360.3 10.1 copy-start.9
  361.0 9.4 slice-start.1
  370.3 4.0 copy-start.8
  385.5 222.1 %reduce-scatter.12.cloned.1.call-start = ((), (), s32[]{:S(2)}) async-start(), calls=%async_computation.12 | async-start | bytes 6488064 | tf_op jit(solution)/shard_map/reduce_scatter | solution.py:337
  410.8 3.7 copy-start.1
  426.8 6.1 copy-start.18
  426.8 6.1 copy-start.20
  438.7 293.6 %reduce-scatter.8.cloned.1.call-start = ((), (), s32[]{:S(2)}) async-start(), calls=%async_computation.10 | async-start | bytes 7299072 | tf_op jit(solution)/shard_map/reduce_scatter | solution.py:335
  447.0 427.8 %reduce-scatter.16.cloned.1.call-start = ((), (), s32[]{:S(2)}) async-start(), calls=%async_computation.14 | async-start | bytes 9732096 | tf_op jit(solution)/shard_map/reduce_scatter | solution.py:286
  456.7 559.0 %reduce-scatter.14.cloned.1.call-start = ((), (), s32[]{:S(2)}) async-start(), calls=%async_computation.13 | async-start | bytes 9732096 | tf_op jit(solution)/shard_map/reduce_scatter | solution.py:285
  465.4 10.7 %copy-start.16 = (f32[768]{0:T(1024)S(1)}, f32[768]{0:T(1024)}, u32[]{:S(2)}) copy-start(f32[768]{0:T(1024)} %get-tuple-element.269) | copy-start | bytes 9220
  465.4 10.8 %copy-start.15 = (f32[768]{0:T(1024)S(1)}, f32[768]{0:T(1024)}, u32[]{:S(2)}) copy-start(f32[768]{0:T(1024)} %get-tuple-element.273) | copy-start | bytes 9220
  (7 other events, 16.6 us)
Sparse Core Ops, SparseCore 0:
  10.9 61.8 all-gather.7
  75.7 58.9 all-gather.9
  137.7 53.0 all-gather.11
  193.5 63.2 all-gather.13
  259.6 62.2 all-gather.15
  385.6 99.9 reduce-scatter.9
  492.8 114.7 reduce-scatter.11
  613.8 118.4 reduce-scatter.7
  739.8 134.9 reduce-scatter.15
  881.1 134.6 reduce-scatter.13
where the time goes:
time: 1030 us; the launch traced here: 1020 us
  waiting for transfers between devices  430 us (42%)
  matrix products  279 us (27%)
  blocking collectives  217 us (21%)
  local copies, waits for them, and re-layouts  47.1 us (5%)
  other arithmetic  33.7 us (3%)
  between operations  14.9 us (1%)
    reduce_scatter x1, waiting for transfers between devices, on_device(): lax.psum_scatter(grad_ff_out, ('dp', 'fsdp'), scatter_dimension=0, tiled=...  142 us
    reduce_scatter x1, waiting for transfers between devices, on_device(): lax.psum_scatter(grad_ff_in, ('dp', 'fsdp'), scatter_dimension=0, tiled=T...  141 us
    reduce_scatter x1, waiting for transfers between devices, on_device(): lax.psum_scatter(grad_qkv, ('dp', 'fsdp'), scatter_dimension=0, tiled=True)  125 us
    unnamed x2, blocking collectives  83.6 us
    all_gather x1, blocking collectives, on_device(): lax.all_gather(biases, ('dp', 'fsdp'), axis=1, tiled=True)  70.6 us
    all_gather x1, blocking collectives, on_device(): lax.all_gather(norm_gains, ('dp', 'fsdp'), axis=1, tiled=True)  63 us
    dot_general x3, matrix products, page_one_third(): jnp.einsum('qkb,bh->hqk', first, bias_table[:B1], preferred_element_type=...  28.4 us
    dot_general x3, matrix products, page_one_third(): jnp.einsum('qkb,bh->hqk', across, bias_table[B1:B1 + B2], preferred_eleme...  22.7 us
  transfers between devices with their start and end apart: 10, of which 4 were waited for; matrix products, arithmetic and copies ran while one was open for 32% of the time, Pallas kernels for 0%

commit v1 on v0

v1 whole, which is shorter than its diff:
```python
from functools import partial

import jax
import jax.numpy as jnp
from jax import lax
from jax.experimental import pallas as pl
from jax.experimental.pallas import tpu as pltpu
from jax.sharding import PartitionSpec as P

HEADS = 12
HEAD_DIM = 64
B1 = 32
B2 = 64
PAIR = 2 * HEAD_DIM
EPSILON = 1e-05
AXES = ("dp", "fsdp")
VMEM_LIMIT = 58 * 2**20
NEVER = -1e30
OUTSIDE = -4096

bf16 = jnp.bfloat16
f32 = jnp.float32


def dot(a, b):
    return jnp.dot(a, b, preferred_element_type=f32)


def dot_nt(a, b):
    return lax.dot_general(a, b, (((1,), (1,)), ((), ())), preferred_element_type=f32)


def dot_tn(a, b):
    return lax.dot_general(a, b, (((0,), (0,)), ((), ())), preferred_element_type=f32)


def params():
    return pltpu.CompilerParams(vmem_limit_bytes=VMEM_LIMIT)


def cost(flops, moved):
    return pl.CostEstimate(flops=int(flops), bytes_accessed=int(moved), transcendentals=0)


def full(shape):
    return pl.BlockSpec(shape, lambda *_: (0,) * len(shape))


def bias_kernel(live, index_ref, table_ref, out_ref):
    rows, width = out_ref.shape[1:]
    first_row = pl.program_id(0) * rows
    tables = [jnp.broadcast_to(table_ref[r : r + 1, :], (8, 128)) for r in range(2 * HEADS)]

    def eight_rows(step, carry):
        at = pl.multiple_of(step * 8, 8)
        key_ids = first_row + at + lax.broadcasted_iota(jnp.int32, (8, 128), 0)
        dead = jnp.where(key_ids < live, 0.0, NEVER)
        for left in range(0, width, 128):
            packed = index_ref[pl.ds(at, 8), left : left + 128]
            flat = packed & (B1 - 1)
            across = (lax.shift_right_logical(packed, 5) & (B2 - 1)) + B1
            downward = lax.shift_right_logical(packed, 11)
            for head in range(HEADS):
                low, high = tables[2 * head], tables[2 * head + 1]
                looked = (
                    jnp.take_along_axis(low, flat, axis=1, mode="promise_in_bounds")
                    + jnp.take_along_axis(low, across, axis=1, mode="promise_in_bounds")
                    + jnp.take_along_axis(high, downward, axis=1, mode="promise_in_bounds")
                    + dead
                )
                right = min(left + 128, width)
                out_ref[head, pl.ds(at, 8), left:right] = looked[:, : right - left]
        return carry

    lax.fori_loop(0, rows // 8, eight_rows, 0)


def score_bias(packed, rel_table, live):
    keys = width = packed.shape[0]
    rows = 64
    lookup = jnp.zeros((HEADS, 2, 128), f32)
    lookup = lookup.at[:, 0, : B1 + B2].set(rel_table[: B1 + B2].T.astype(f32))
    lookup = lookup.at[:, 1, :B2].set(rel_table[B1 + B2 :].T.astype(f32))
    return pl.pallas_call(
        partial(bias_kernel, live),
        grid=(keys // rows,),
        in_specs=[pl.BlockSpec((rows, packed.shape[1]), lambda i: (i, 0)), full((2 * HEADS, 128))],
        out_specs=pl.BlockSpec((HEADS, rows, width), lambda i: (0, i, 0)),
        out_shape=jax.ShapeDtypeStruct((HEADS, keys, width), f32),
        compiler_params=params(),
        cost_estimate=cost(3e10, 4 * HEADS * keys * width),
    )(packed, lookup.reshape(2 * HEADS, 128))


def embed_kernel(token_ref, place_ref, table_ref, weight_ref, small_ref, begin_ref, rows_ref, united_ref):
    half = table_ref.shape[0] // 2
    width = token_ref.shape[1]
    columns = lax.broadcasted_iota(jnp.int32, (token_ref.shape[0], half), 1)
    total = token_ref[...].astype(f32)
    for side in range(2):
        hot = jnp.where(place_ref[:, side : side + 1] == columns, 1.0, 0.0).astype(bf16)
        total += dot(hot, table_ref[side * half : (side + 1) * half, :])
    begin_ref[...] = total
    rows = total.astype(bf16)
    rows_ref[...] = rows
    query = dot(rows, weight_ref[:, :width]) + small_ref[0:1, :]
    united_ref[:, :width] = (query * 0.125).astype(bf16)
    united_ref[:, width : 2 * width] = dot(rows, weight_ref[:, width : 2 * width]).astype(bf16)
    value = dot(rows, weight_ref[:, 2 * width :]) + small_ref[1:2, :]
    united_ref[:, 2 * width :] = value.astype(bf16)


def embed(tokens, places, dcpe_table, w_qkv, small):
    count, width = tokens.shape
    return pl.pallas_call(
        embed_kernel,
        out_shape=(
            jax.ShapeDtypeStruct((count, width), f32),
            jax.ShapeDtypeStruct((count, width), bf16),
            jax.ShapeDtypeStruct((count, 3 * width), bf16),
        ),
        compiler_params=params(),
        cost_estimate=cost(2 * count * width * (dcpe_table.shape[0] + 3 * width), 12e6),
    )(tokens, places, dcpe_table, w_qkv, small)


def head_mask(head):
    return lax.broadcasted_iota(jnp.int32, (1, PAIR), 1) // HEAD_DIM == head


def attend_kernel(query_ref, key_ref, value_ref, bias_ref, attention_ref, context_ref):
    query, key = query_ref[...], key_ref[...]
    value_t = value_ref[...].astype(f32).T.astype(bf16)
    parts = []
    for head in range(2):
        scores = dot_nt(jnp.where(head_mask(head), key, 0), query) + bias_ref[head]
        raised = jnp.exp(scores - jnp.max(scores, axis=0, keepdims=True))
        attention = (raised * (1.0 / jnp.sum(raised, axis=0, keepdims=True))).astype(bf16)
        attention_ref[head] = attention
        parts.append(dot(value_t[head * HEAD_DIM : (head + 1) * HEAD_DIM], attention))
    context_ref[...] = jnp.concatenate(parts, axis=0).T.astype(bf16)


def attend(united, bias):
    count = united.shape[0]
    pairs = HEADS // 2
    column = lambda shift: pl.BlockSpec((count, PAIR), lambda p: (0, p + shift))
    square = pl.BlockSpec((2, count, count), lambda p: (p, 0, 0))
    return pl.pallas_call(
        attend_kernel,
        grid=(pairs,),
        in_specs=[column(0), column(pairs), column(2 * pairs), square],
        out_specs=(square, column(0)),
        out_shape=(
            jax.ShapeDtypeStruct((HEADS, count, count), bf16),
            jax.ShapeDtypeStruct((count, HEADS * HEAD_DIM), bf16),
        ),
        compiler_params=params(),
        cost_estimate=cost(4 * HEADS * count * count * HEAD_DIM, 6 * HEADS * count * count),
    )(united, united, united, bias)


def attend_back_kernel(
    query_ref, key_ref, value_ref, attention_ref, d_context_ref, d_query_ref, d_key_ref, d_value_ref, d_scores_ref
):
    query, value, d_context = query_ref[...], value_ref[...], d_context_ref[...]
    key_t = key_ref[...].astype(f32).T.astype(bf16)
    parts = []
    d_key = jnp.zeros(query.shape, f32)
    d_value = jnp.zeros(query.shape, f32)
    for head in range(2):
        mask = head_mask(head)
        d_attention = dot_nt(jnp.where(mask, value, 0), d_context)
        attention_low = attention_ref[head]
        attention = attention_low.astype(f32)
        centre = jnp.sum(attention * d_attention, axis=0, keepdims=True)
        d_scores = (attention * (d_attention - centre)).astype(bf16)
        d_scores_ref[head] = d_scores
        d_key += dot(d_scores, jnp.where(mask, query, 0))
        d_value += dot(attention_low, jnp.where(mask, d_context, 0))
        parts.append(dot(key_t[head * HEAD_DIM : (head + 1) * HEAD_DIM], d_scores))
    d_query_ref[...] = jnp.concatenate(parts, axis=0).T.astype(bf16) * bf16(0.125)
    d_key_ref[...] = d_key.astype(bf16)
    d_value_ref[...] = d_value.astype(bf16)


def attend_back(united, attention, d_context):
    count = united.shape[0]
    pairs = HEADS // 2
    column = lambda shift: pl.BlockSpec((count, PAIR), lambda p: (0, p + shift))
    square = pl.BlockSpec((2, count, count), lambda p: (p, 0, 0))
    joined = jax.ShapeDtypeStruct((count, HEADS * HEAD_DIM), bf16)
    return pl.pallas_call(
        attend_back_kernel,
        grid=(pairs,),
        in_specs=[column(0), column(pairs), column(2 * pairs), square, column(0)],
        out_specs=(column(0), column(0), column(0), square),
        out_shape=(joined, joined, joined, jax.ShapeDtypeStruct((HEADS, count, count), bf16)),
        compiler_params=params(),
        cost_estimate=cost(8 * HEADS * count * count * HEAD_DIM, 4 * HEADS * count * count),
    )(united, united, united, attention, d_context)


def unit_rows(values):
    centred = values - jnp.mean(values, axis=1, keepdims=True)
    scale = lax.rsqrt(jnp.mean(centred * centred, axis=1, keepdims=True) + EPSILON)
    return centred * scale, scale


def unit_rows_back(units, scale, d_units):
    spread = jnp.mean(d_units * units, axis=1, keepdims=True)
    return scale * (d_units - jnp.mean(d_units, axis=1, keepdims=True) - units * spread)


def column_sum(values):
    return jnp.sum(values.astype(f32), axis=0, keepdims=True)


def middle_kernel(
    live,
    tile,
    begin_ref,
    context_ref,
    w_out_ref,
    w_in_ref,
    w_back_ref,
    small_ref,
    hidden_bias_ref,
    slot_ref,
    slot_grad_ref,
    layer_ref,
    g_in_ref,
    g_back_ref,
    g_out_ref,
    d_pre_ref,
    d_context_ref,
    sums_ref,
    hidden_sum_ref,
    act_ref,
    slope_ref,
    rows_t_ref,
):
    count, width = begin_ref.shape
    hidden = w_back_ref.shape[0]
    tiles = hidden // tile
    row = lambda i: small_ref[i : i + 1, :]
    attended = dot(context_ref[...], w_out_ref[...]) + row(2)
    units, scale = unit_rows(begin_ref[...] + attended)
    mid = units * row(6) + row(3)
    mid_rows = mid.astype(bf16)
    rows_t_ref[...] = mid.T.astype(bf16)

    def forward_tile(step, total):
        at = pl.ds(pl.multiple_of(step * tile, tile), tile)
        inner = dot(mid_rows, w_in_ref[:, at]) + hidden_bias_ref[:, at]
        share = 0.5 * lax.erf(inner * (2.0**-0.5)) + 0.5
        bell = jnp.exp(inner * inner * -0.5) * (0.5 * 2.0**0.5 / jnp.pi**0.5)
        act = (inner * share).astype(bf16)
        act_ref[:, at] = act
        slope_ref[:, at] = (share + inner * bell).astype(bf16)
        return total + dot(act, w_back_ref[at, :])

    outer = lax.fori_loop(0, tiles, forward_tile, jnp.zeros((count, width), f32))
    out_units, out_scale = unit_rows(mid + outer + row(4))
    layer_ref[...] = (out_units * row(7) + row(5)).astype(bf16)

    token_ids = lax.broadcasted_iota(jnp.int32, (count, slot_ref.shape[1]), 0)
    slot_hot = jnp.where(slot_ref[...] == token_ids, 1.0, 0.0).astype(bf16)
    out_cot = dot(slot_hot, slot_grad_ref[...])
    d_sum = unit_rows_back(out_units, out_scale, out_cot * row(7))
    d_outer = d_sum.astype(bf16)

    def backward_tile(step, total):
        at = pl.ds(pl.multiple_of(step * tile, tile), tile)
        d_act = dot_nt(d_outer, w_back_ref[at, :])
        d_inner = (d_act * slope_ref[:, at].astype(f32)).astype(bf16)
        g_back_ref[at, :] = dot_tn(act_ref[:, at], d_outer).astype(bf16)
        g_in_ref[:, at] = dot(rows_t_ref[...], d_inner).astype(bf16)
        hidden_sum_ref[:, at] = column_sum(d_inner)
        return total + dot_nt(d_inner, w_in_ref[:, at])

    d_mid = lax.fori_loop(0, tiles, backward_tile, d_sum)
    d_pre = unit_rows_back(units, scale, d_mid * row(6))
    d_pre_ref[...] = d_pre
    d_att = d_pre.astype(bf16)
    g_out_ref[...] = dot_tn(context_ref[...], d_att).astype(bf16)
    d_context_ref[...] = dot_nt(d_att, w_out_ref[...]).astype(bf16)
    sums_ref[0:1, :] = column_sum(d_att)
    sums_ref[1:2, :] = column_sum(d_mid)
    sums_ref[2:3, :] = column_sum(d_outer)
    sums_ref[3:4, :] = column_sum(out_cot)
    sums_ref[4:5, :] = column_sum(d_mid * units)
    sums_ref[5:6, :] = column_sum(out_cot * out_units)
    sums_ref[6:8, :] = jnp.zeros((2, width), f32)


def middle(live, begin, context, w_attn_out, w_ff_in, w_ff_out, small, hidden_bias, slots, slot_grads):
    count, width = begin.shape
    hidden = w_ff_out.shape[0]
    return pl.pallas_call(
        partial(middle_kernel, live, 512),
        out_shape=(
            jax.ShapeDtypeStruct((count, width), bf16),
            jax.ShapeDtypeStruct((width, hidden), bf16),
            jax.ShapeDtypeStruct((hidden, width), bf16),
            jax.ShapeDtypeStruct((width, width), bf16),
            jax.ShapeDtypeStruct((count, width), f32),
            jax.ShapeDtypeStruct((count, width), bf16),
            jax.ShapeDtypeStruct((8, width), f32),
            jax.ShapeDtypeStruct((1, hidden), f32),
        ),
        scratch_shapes=[
            pltpu.VMEM((count, hidden), bf16),
            pltpu.VMEM((count, hidden), bf16),
            pltpu.VMEM((width, count), bf16),
        ],
        compiler_params=params(),
        cost_estimate=cost(12 * count * width * hidden, 30e6),
    )(begin, context, w_attn_out, w_ff_in, w_ff_out, small, hidden_bias, slots, slot_grads)


def embed_back_kernel(
    d_query_ref,
    d_key_ref,
    d_value_ref,
    weight_ref,
    d_pre_ref,
    rows_ref,
    place_ref,
    input_grad_ref,
    g_qkv_ref,
    g_table_ref,
    sums_ref,
):
    count, width = rows_ref.shape
    rows_t = rows_ref[...].astype(f32).T.astype(bf16)
    total = d_pre_ref[...]
    for part, d_ref in enumerate((d_query_ref, d_key_ref, d_value_ref)):
        at = slice(part * width, (part + 1) * width)
        total += dot_nt(d_ref[...], weight_ref[:, at])
        g_qkv_ref[:, at] = dot(rows_t, d_ref[...]).astype(bf16)
    input_grad_ref[...] = total
    low = total.astype(bf16)
    half = g_table_ref.shape[0] // 2
    values = lax.broadcasted_iota(jnp.int32, (half, count), 0)
    for side in range(2):
        hot = jnp.where(place_ref[side : side + 1, :] == values, 1.0, 0.0).astype(bf16)
        g_table_ref[side * half : (side + 1) * half, :] = dot(hot, low).astype(bf16)
    sums_ref[0:1, :] = column_sum(d_query_ref[...])
    sums_ref[1:2, :] = column_sum(d_value_ref[...])
    sums_ref[2:8, :] = jnp.zeros((6, width), f32)


def embed_back(d_query, d_key, d_value, w_qkv, d_pre, begin_rows, places, table_rows):
    count, width = begin_rows.shape
    return pl.pallas_call(
        embed_back_kernel,
        out_shape=(
            jax.ShapeDtypeStruct((count, width), f32),
            jax.ShapeDtypeStruct((width, 3 * width), bf16),
            jax.ShapeDtypeStruct((table_rows, width), bf16),
            jax.ShapeDtypeStruct((8, width), f32),
        ),
        compiler_params=params(),
        cost_estimate=cost(2 * count * width * (table_rows + 6 * width), 20e6),
    )(d_query, d_key, d_value, w_qkv, d_pre, begin_rows, places)


GROUP = 8
TABLES = ((0, B1), (5, B2), (11, B2))


def table_kernel(index_ref, d_scores_ref, out_ref, total_ref):
    keys, count = d_scores_ref.shape[1:]
    columns = 2 * HEADS * GROUP

    @pl.when(pl.program_id(0) == 0)
    def _():
        total_ref[...] = jnp.zeros_like(total_ref)

    d_scores = d_scores_ref[...].astype(f32)
    packed = index_ref[:, :count]
    base = 0
    for shift, buckets in TABLES:
        bucket = lax.shift_right_logical(packed, shift) & (buckets - 1)
        upper, lowest = lax.shift_right_logical(bucket, 1), bucket & 1
        uppers = buckets // 2
        values = lax.broadcasted_iota(jnp.int32, (uppers, count), 0)
        left, right = [], []
        for first in range(0, keys, GROUP):
            group = slice(first, first + GROUP)
            left.append(
                jnp.concatenate(
                    [jnp.where(upper[k : k + 1] == values, 1.0, 0.0).astype(bf16) for k in range(first, first + GROUP)],
                    axis=0,
                )
            )
            right.append(
                jnp.concatenate(
                    [
                        jnp.where((lowest[group] == bit)[None], d_scores[:, group, :], 0.0).reshape(
                            HEADS * GROUP, count
                        )
                        for bit in range(2)
                    ],
                    axis=0,
                ).astype(bf16)
            )
        total_ref[base : base + uppers * GROUP, :] += dot_nt(
            jnp.concatenate(left, axis=1), jnp.concatenate(right, axis=1)
        )
        base += uppers * GROUP

    @pl.when(pl.program_id(0) == pl.num_programs(0) - 1)
    def _():
        base, pieces = 0, []
        for _, buckets in TABLES:
            shape = (GROUP, buckets // 2, columns)
            block = total_ref[base : base + shape[0] * shape[1], :].reshape(shape)
            own = lax.broadcasted_iota(jnp.int32, shape, 2) % GROUP == lax.broadcasted_iota(jnp.int32, shape, 0)
            pieces.append(jnp.sum(jnp.where(own, block, 0.0), axis=0))
            base += shape[0] * shape[1]
        out_ref[...] = jnp.concatenate(pieces, axis=0)


def table_grad(packed, d_scores):
    count = packed.shape[0]
    keys = 32
    uppers = (B1 + 2 * B2) // 2
    columns = 2 * HEADS * GROUP
    folded = pl.pallas_call(
        table_kernel,
        grid=(count // keys,),
        in_specs=[
            pl.BlockSpec((keys, packed.shape[1]), lambda i: (i, 0)),
            pl.BlockSpec((HEADS, keys, count), lambda i: (0, i, 0)),
        ],
        out_specs=full((uppers, columns)),
        out_shape=jax.ShapeDtypeStruct((uppers, columns), f32),
        scratch_shapes=[pltpu.VMEM((uppers * GROUP, columns), f32)],
        compiler_params=params(),
        cost_estimate=cost(2e10, 2 * HEADS * count * count),
    )(packed, d_scores)
    return folded.reshape(uppers, 2, HEADS, GROUP).sum(axis=3).reshape(2 * uppers, HEADS)


def swap(values, bit, devices):
    return lax.ppermute(values, AXES, [(i, i ^ bit) for i in range(devices)])


def reduce_blocks(blocks, bits, index, devices):
    order = []
    width = devices
    open_bits = []
    b = 1
    while b < devices:
        open_bits.append(b)
        b *= 2
    for bit in bits:
        place = open_bits.index(bit)
        inner = 2**place
        outer = 2 ** (len(open_bits) - 1 - place)
        view = blocks.reshape((outer, 2, inner) + blocks.shape[1:])
        mine = (index // bit) % 2
        away = lax.dynamic_index_in_dim(view, 1 - mine, axis=1, keepdims=False)
        keep = lax.dynamic_index_in_dim(view, mine, axis=1, keepdims=False)
        came = swap(away, bit, devices)
        summed = (keep.astype(f32) + came.astype(f32)).astype(blocks.dtype)
        blocks = summed.reshape((outer * inner,) + blocks.shape[1:])
        open_bits.pop(place)
    return blocks[0]


def sum_everywhere(values, bits, devices):
    for bit in bits:
        values = values + swap(values, bit, devices)
    return values


def to_blocks(grad, devices, width):
    rows, columns = grad.shape
    parts = columns // width
    blocks = grad.reshape(devices, rows // devices, parts, width)
    return blocks.transpose(0, 2, 1, 3).reshape(devices, parts * (rows // devices), width)


def from_block(block, parts):
    rows, width = block.shape
    return block.reshape(parts, rows // parts, width).transpose(1, 0, 2).reshape(rows // parts, parts * width)


def from_blocks(blocks, parts):
    devices, rows, width = blocks.shape
    split = blocks.reshape(devices, parts, rows // parts, width)
    return split.transpose(0, 2, 1, 3).reshape(devices * (rows // parts), parts * width)


def on_device(
    devices,
    bits,
    tokens,
    coords,
    rel_pos,
    rel_box,
    entity_pairs,
    entity_grad,
    w_qkv,
    w_attn_out,
    dcpe_table,
    biases,
    norm_gains,
    w_ff_in,
    w_ff_out,
    ff_bias,
    rel_table,
):
    live, width = tokens.shape[1], tokens.shape[2]
    hidden = ff_bias.shape[0] * devices
    count = -(-live // 64) * 64
    extra = count - live
    index = lax.axis_index(AXES)
    shard = biases.shape[1]

    small_own = jnp.zeros((8, width), bf16)
    small_own = small_own.at[:6, :shard].set(biases).at[6:8, :shard].set(norm_gains)
    small_own = small_own.at[0, 128 : 128 + ff_bias.shape[0]].set(ff_bias)
    first_own = jnp.concatenate([from_block_rows(w_qkv, width), w_attn_out, dcpe_table, small_own], axis=0)
    second_own = jnp.concatenate([from_block_rows(w_ff_in, width), w_ff_out], axis=0)
    first = lax.all_gather(first_own, AXES, axis=0)
    second = lax.all_gather(second_own, AXES, axis=0)

    packed = rel_pos[0] + rel_box[0, 0] * 32 + rel_box[0, 1] * 2048
    packed = jnp.pad(packed.T, ((0, extra), (0, -(-count // 128) * 128 - live)))
    bias = score_bias(packed, rel_table, live)
    places = jnp.pad(coords[0], ((0, 0), (0, extra)), constant_values=OUTSIDE)
    slots = entity_pairs.reshape(1, -1)
    slot_grads = entity_grad.reshape(slots.shape[1], width)
    padded = jnp.pad(tokens[0], ((0, extra), (0, 0)))

    q_rows, o_rows, t_rows = 3 * w_qkv.shape[0], w_attn_out.shape[0], dcpe_table.shape[0]
    full_qkv = from_blocks(first[:, :q_rows], 3)
    full_out = first[:, q_rows : q_rows + o_rows].reshape(width, width)
    full_table = first[:, q_rows + o_rows : q_rows + o_rows + t_rows].reshape(-1, width)
    small_all = first[:, q_rows + o_rows + t_rows :]
    small = small_all[:, :, :shard].transpose(1, 0, 2).reshape(8, width).astype(f32)
    hidden_bias = small_all[:, 0, 128 : 128 + ff_bias.shape[0]].reshape(1, hidden).astype(f32)
    f_rows = second_own.shape[0] - w_ff_out.shape[0]
    full_in = from_blocks(second[:, :f_rows], hidden // width)
    full_back = second[:, f_rows:].reshape(hidden, width)

    begin, begin_rows, united = embed(padded, places.T, full_table, full_qkv, small)
    attention, context = attend(united, bias)
    layer_out, g_in, g_back, g_out, d_pre, d_context, sums, hidden_sum = middle(
        live, begin, context, full_out, full_in, full_back, small, hidden_bias, slots, slot_grads
    )
    ff_blocks = jnp.concatenate([to_blocks(g_in, devices, width), g_back.reshape(devices, -1, width)], axis=1)
    ff_own = reduce_blocks(ff_blocks, bits, index, devices)

    d_query, d_key, d_value, d_scores = attend_back(united, attention, d_context)
    input_grad, g_qkv, g_table, more_sums = embed_back(
        d_query, d_key, d_value, full_qkv, d_pre, begin_rows, places, full_table.shape[0]
    )
    grads = jnp.concatenate([more_sums[:2], sums[:6]], axis=0)
    small_blocks = jnp.zeros((devices, 8, width), bf16)
    small_blocks = small_blocks.at[:, :, :shard].set(grads.reshape(8, devices, shard).transpose(1, 0, 2).astype(bf16))
    small_blocks = small_blocks.at[:, 0, 128 : 128 + ff_bias.shape[0]].set(
        hidden_sum.reshape(devices, ff_bias.shape[0]).astype(bf16)
    )
    blocks = jnp.concatenate(
        [
            to_blocks(g_qkv, devices, width),
            g_out.reshape(devices, -1, width),
            g_table.reshape(devices, -1, width),
            small_blocks,
        ],
        axis=1,
    )
    own = reduce_blocks(blocks, bits, index, devices).astype(f32)
    table_sum = sum_everywhere(table_grad(packed, d_scores), bits, devices)
    small_sum = own[q_rows + o_rows + t_rows :]
    ff_own = ff_own.astype(f32)
    return (
        layer_out[None, :live],
        input_grad[None, :live],
        from_block(own[:q_rows], 3),
        own[q_rows : q_rows + o_rows],
        own[q_rows + o_rows : q_rows + o_rows + t_rows],
        small_sum[:6, :shard],
        small_sum[6:8, :shard],
        from_block(ff_own[:f_rows], hidden // width),
        ff_own[f_rows:],
        small_sum[0, 128 : 128 + ff_bias.shape[0]],
        table_sum,
    )


def from_block_rows(shard, width):
    rows, columns = shard.shape
    return shard.reshape(rows, columns // width, width).transpose(1, 0, 2).reshape(-1, width)


def solution(mesh):
    outer, inner = mesh.shape["dp"], mesh.shape["fsdp"]
    devices = outer * inner
    bits = [inner] + [1 << k for k in range(devices.bit_length() - 1) if 1 << k != inner]
    rows = P(AXES, None)
    three = P(AXES, None, None)
    four = P(AXES, None, None, None)
    columns = P(None, AXES)
    return jax.shard_map(
        partial(on_device, devices, bits),
        mesh=mesh,
        in_specs=(three, three, three, four, three, four, rows, rows, rows, columns, columns, rows, rows, P(AXES), P()),
        out_specs=(three, three, rows, rows, rows, columns, columns, rows, rows, P(AXES), P()),
        check_vma=False,
    )
```

time: 1030 us -> 517 us (0.50)
  matrix products: 279 us -> 0 us
  waiting for transfers between devices: 430 us -> 166 us
  blocking collectives: 217 us -> 0 us
  Pallas kernels: 0 us -> 158 us
  local copies, waits for them, and re-layouts: 47.1 us -> 115 us
  starting transfers between devices: 0.39 us -> 13.2 us
  other arithmetic: 33.7 us -> 44.7 us
    reduce_scatter x5 -> x0, waiting for transfers between devices: 426 us -> none  [the longest x1 142 us: on_device(): lax.psum_scatter(grad_ff_out, ('dp', 'fsdp'), scatter_dimension=0, tiled=...]
    dot_general x39 -> x0, matrix products: 279 us -> none  [the longest x3 28.4 us: page_one_third(): jnp.einsum('qkb,bh->hqk', first, bias_table[:B1], preferred_element_type=...]
    pallas_call x0 -> x7, Pallas kernels: none -> 158 us  [the longest x1 39.4 us: score_bias(): pl.pallas_call(partial(bias_kernel, live), grid=(keys // rows,), in_specs...]
    all_gather x2 -> x0, blocking collectives: 134 us -> none  [the longest x1 70.6 us: on_device(): lax.all_gather(biases, ('dp', 'fsdp'), axis=1, tiled=True)]
    ppermute x0 -> x15, waiting for transfers between devices: none -> 113 us  [swap(): return lax.ppermute(values, AXES, [(i, i ^ bit) for i in range(devices)])]
    unnamed x2 -> x0, blocking collectives: 83.6 us -> none
    all_gather x5 -> x2, waiting for transfers between devices: 0.05 us -> 53.2 us  [the longest x1 42.6 us: on_device(): second = lax.all_gather(second_own, AXES, axis=0)]
    slice x4 -> x13, local copies, waits for them, and re-layouts: 3.18 us -> 25.3 us  [the longest x1 6.54 us: on_device(): full_back = second[:, f_rows:].reshape(hidden, width)]
  transfers between devices with their start and end apart: 10 -> 17, of which waited for: 4 -> 12; matrix products, arithmetic and copies ran while one was open for 32% -> 18% of each run, Pallas kernels for 0% -> 18%
where the time goes in v1:
time: 517 us; the launch traced here: 511 us
  waiting for transfers between devices  166 us (32%)
  Pallas kernels  158 us (31%)
  local copies, waits for them, and re-layouts  115 us (22%)
  other arithmetic  44.7 us (9%)
  between operations  14.7 us (3%)
  starting transfers between devices  13.2 us (3%)
    ppermute x15, waiting for transfers between devices, swap(): return lax.ppermute(values, AXES, [(i, i ^ bit) for i in range(devices)])  113 us
    all_gather x1, waiting for transfers between devices, on_device(): second = lax.all_gather(second_own, AXES, axis=0)  42.6 us
    pallas_call x1, Pallas kernels, score_bias(): pl.pallas_call(partial(bias_kernel, live), grid=(keys // rows,), in_specs...  39.4 us
    pallas_call x1, Pallas kernels, middle(): pl.pallas_call(partial(middle_kernel, live, 512), out_shape=(jax.ShapeDty...  38.3 us
    unnamed x45, local copies, waits for them, and re-layouts  25.7 us
    pallas_call x1, Pallas kernels, table_grad(): pl.pallas_call(table_kernel, grid=(count // keys,), in_specs=[pl.BlockSpe...  25.3 us
    reshape x3, local copies, waits for them, and re-layouts, to_blocks(): blocks = grad.reshape(devices, rows // devices, parts, width)  23.9 us
    convert_element_type x8, other arithmetic, reduce_blocks(): summed = (keep.astype(f32) + came.astype(f32)).astype(blocks.dtype)  21.5 us
  transfers between devices with their start and end apart: 17, of which 12 were waited for; matrix products, arithmetic and copies ran while one was open for 18% of the time, Pallas kernels for 18%

profile of v1, /device:TPU:0, one launch (start us, length us, event | category | flops | bytes accessed | tf_op | source)
XLA Modules:
  0.0 511.4 jit_solution(11657629169727375738)
XLA Ops:
  25.0 6.3 %fusion.16 = (s32[1,1,561,561]{3,1,2,0:T(1,128)S(1)}, s32[1,1,561,561]{3,1,2,0:T(1,128)}) fusion(s32[1,2,561,561]{3,1,2,0:T(2,128)} %param.32), kind=kLoop, calls=%fused_computation.66 | loop fusion | bytes 5035536 | tf_op jit(solution)/shard_map/slice | solution.py:532
  33.6 3.5 copy.123
  37.2 4.4 copy.105
  47.6 39.4 %shard_map.231.bias_ref = f32[12,576,576]{2,1,0:T(8,128)} custom-call(s32[576,640]{1,0:T(8,128)} %pad.44.index_ref, f32[24,128]{1,0:T(8,128)} %bitcast.183), custom_call_target="tpu_custom_call" | custom-call | flops 30000001024 | bytes 15925248 | tf_op jit(solution)/shard_map/pallas_call | solution.py:84
  87.0 10.6 %all-gather.5.cloned.1.call-done = bf16[5376,768]{1,0:T(8,128)(2,1)} async-done(((bf16[168,768]{1,0:T(8,128)(2,1)}), bf16[5376,768]{1,0:T(8,128)(2,1)}) %all-gather.5.cloned.1.call-update) | async-done | bytes 8257552 | tf_op jit(solution)/shard_map/all_gather | solution.py:529
  99.9 3.9 slice.278
  114.2 9.9 %shard_map.230 = (f32[576,768]{1,0:T(8,128)}, bf16[576,768]{1,0:T(8,128)(2,1)}, bf16[576,2304]{1,0:T(8,128)(2,1)}) custom-call(bf16[576,768]{1,0:T(8,128)(2,1)} %pad.42.token_ref, s32[576,2]{1,0:T(8,128)} %copy.104.place_ref, bf16[2048,768]{1,0:T(8,128)(2,1)} %bitcast.160, bf16[768,2304]{1,0:T(8,128)(2,1)} %bitcast.158, f32[8,768]{1,0:T(8,128)} %reshape.487.small_ref), custom_call_target="tpu_custom_call" | custom-call | flops 3850371072 | bytes 12000000 | tf_op jit(solution)/shard_map/pallas_call | solution.py:115
  124.1 15.2 %shard_map.232 = (bf16[12,576,576]{2,1,0:T(8,128)(2,1)}, bf16[576,768]{1,0:T(8,128)(2,1)}) custom-call(bf16[576,2304]{1,0:T(8,128)(2,1)} %get-tuple-element.117.query_ref.key_ref.value_ref, bf16[576,2304]{1,0:T(8,128)(2,1)} %get-tuple-element.117.query_ref.key_ref.value_ref, bf16[576,2304]{1,0:T(8,128)(2,1)} %get-tuple-element.117.query_ref.key_ref.value_ref, ...), custom_call_target="tpu_custom_call" | custom-call | flops 1019215872 | bytes 23887872 | tf_op jit(solution)/shard_map/pallas_call | solution.py:149
  139.3 42.6 %all-gather.7.cloned.1.call-done = bf16[6144,768]{1,0:T(8,128)(2,1)} async-done(((bf16[192,768]{1,0:T(8,128)(2,1)}), bf16[6144,768]{1,0:T(8,128)(2,1)}) %all-gather.7.cloned.1.call-update) | async-done | bytes 9437200 | tf_op jit(solution)/shard_map/all_gather | solution.py:530
  181.9 6.5 %fusion.15 = (bf16[32,96,768]{2,1,0:T(8,128)(2,1)}, bf16[32,96,768]{2,1,0:T(8,128)(2,1)S(1)}) fusion(bf16[32,192,768]{2,1,0:T(8,128)(2,1)} %bitcast.144), kind=kLoop, calls=%fused_computation.65 | loop fusion | bytes 18874368 | tf_op jit(solution)/shard_map/slice | solution.py:549
  190.8 3.2 copy.128
  194.0 38.3 %shard_map.233 = (bf16[576,768]{1,0:T(8,128)(2,1)}, bf16[768,3072]{1,0:T(8,128)(2,1)}, bf16[3072,768]{1,0:T(8,128)(2,1)}, bf16[768,768]{1,0:T(8,128)(2,1)}, f32[...) custom-call(f32[576,768]{1,0:T(8,128)} %get-tuple-element.116.begin_ref, ...), custom_call_target="tpu_custom_call" | custom-call | flops 16307453952 | bytes 30000000 | tf_op jit(solution)/shard_map/pallas_call | solution.py:300
  232.3 9.7 %reshape.482 = bf16[32,24,4,768]{3,2,1,0:T(4,128)(2,1)} reshape(bf16[768,3072]{1,0:T(8,128)(2,1)} %get-tuple-element.134) | data formatting | bytes 9437184 | tf_op jit(solution)/shard_map/reshape | solution.py:483
  242.1 5.4 %copy.116 = bf16[32,24,4,768]{3,1,2,0:T(8,128)(2,1)} copy(bf16[32,24,4,768]{3,2,1,0:T(4,128)(2,1)} %reshape.482) | data formatting | bytes 9437184 | tf_op jit(solution)/shard_map/reshape | solution.py:483
  247.5 16.8 %shard_map.234 = (bf16[576,768]{1,0:T(8,128)(2,1)}, bf16[576,768]{1,0:T(8,128)(2,1)}, bf16[576,768]{1,0:T(8,128)(2,1)}, bf16[12,576,576]{2,1,0:T(8,128)(2,1)}) custom-call(bf16[576,2304]{1,0:T(8,128)(2,1)} %get-tuple-element.117.query_ref.key_ref.value_ref, bf16[576,2304]{1,0:T(8,128)(2,1)} %get-tuple-element.117.query_ref.key_ref.value_ref, ...), custom_call_target="tpu_custom_call" | custom-call | flops 2038431744 | bytes 15925248 | tf_op jit(solution)/shard_map/pallas_call | solution.py:193
  264.3 12.8 %shard_map.235 = (f32[576,768]{1,0:T(8,128)}, bf16[768,2304]{1,0:T(8,128)(2,1)}, bf16[2048,768]{1,0:T(8,128)(2,1)}, f32[8,768]{1,0:T(8,128)}) custom-call(bf16[576,768]{1,0:T(8,128)(2,1)} %get-tuple-element.122.d_query_ref, bf16[576,768]{1,0:T(8,128)(2,1)} %get-tuple-element.123.d_key_ref, bf16[576,768]{1,0:T(8,128)(2,1)} %get-tuple-element.124.d_value_ref, ...), custom_call_target="tpu_custom_call" | custom-call | flops 5888802816 | bytes 20000000 | tf_op jit(solution)/shard_map/pallas_call | solution.py:356
  277.1 8.7 %reshape.479 = bf16[32,24,3,768]{3,2,1,0:T(4,128)(2,1)} reshape(bf16[768,2304]{1,0:T(8,128)(2,1)} %get-tuple-element.128) | data formatting | bytes 7077888 | tf_op jit(solution)/shard_map/reshape | solution.py:483
  285.9 4.8 copy.112
  295.5 4.2 pad_maximum_fusion
  304.3 4.3 fusion.3
  309.6 4.8 fusion.1
  319.4 6.7 %fusion = bf16[8,2,192,768]{3,2,1,0:T(8,128)(2,1)} fusion(bf16[8,2,192,768]{3,2,1,0:T(8,128)(2,1)} %collective-permute-done.5, s32[]{:T(128)S(6)} %select_n.104, bf16[8,2,2,96,768]{4,3,2,1,0:T(8,128)(2,1)S(1)} %bitcast.133, bf16[8,2,2,96,768]{4,3,2,1,0:T(8,128)(2,1)} %bitcast.139), kind=kLoop, calls=%fused_computation.5 | loop fusion | flops 18874368 | bytes 18874372 | tf_op jit(solution)/shard_map/convert_element_type | solution.py:468
  328.5 37.4 %collective-permute-done.1 = bf16[8,1,168,768]{3,2,1,0:T(8,128)(2,1)} collective-permute-done((bf16[8,1,168,768]{3,2,1,0:T(8,128)(2,1)}, bf16[8,1,168,768]{3,2,1,0:T(8,128)(2,1)}, u32[]{:S(2)}, u32[]{:S(2)}) %collective-permute-start.1) | collective-permute-done | bytes 2064416 | tf_op jit(solution)/shard_map/ppermute | solution.py:448
  371.5 44.3 %collective-permute-done.6 = bf16[8,1,192,768]{3,2,1,0:T(8,128)(2,1)} collective-permute-done((bf16[8,1,192,768]{3,2,1,0:T(8,128)(2,1)S(1)}, bf16[8,1,192,768]{3,2,1,0:T(8,128)(2,1)}, u32[]{:S(2)}, u32[]{:S(2)}) %collective-permute-start.6) | collective-permute-done | bytes 2359328 | tf_op jit(solution)/shard_map/ppermute | solution.py:448
  415.8 2.9 add_convert_fusion
  425.1 25.3 %shard_map.236 = f32[80,192]{1,0:T(8,128)} custom-call(s32[576,640]{1,0:T(8,128)} %pad.44.index_ref, bf16[12,576,576]{2,1,0:T(8,128)(2,1)} %get-tuple-element.136.d_scores_ref), custom_call_target="tpu_custom_call" | custom-call | flops 20000000000 | bytes 7962624 | tf_op jit(solution)/shard_map/pallas_call | solution.py:431
  453.5 3.9 collective-permute-done.11
  458.1 3.8 collective-permute-done.12
  474.6 3.0 copy.120
  478.3 4.6 collective-permute-done.4
  484.5 5.6 %collective-permute-done.8 = bf16[2,1,192,768]{3,2,0,1:T(8,128)(2,1)S(1)} collective-permute-done((bf16[2,1,192,768]{3,2,0,1:T(8,128)(2,1)S(1)}, bf16[2,1,192,768]{3,2,0,1:T(8,128)(2,1)S(1)}, u32[]{:S(2)}, u32[]{:S(2)}) %collective-permute-start.8) | collective-permute-done | bytes 589856 | tf_op jit(solution)/shard_map/ppermute | solution.py:448
  494.0 8.8 %collective-permute-done.9 = bf16[1,1,192,768]{3,2,0,1:T(8,128)(2,1)S(1)} collective-permute-done((bf16[1,1,192,768]{3,2,0,1:T(8,128)(2,1)S(1)}, bf16[1,1,192,768]{3,2,0,1:T(8,128)(2,1)S(1)}, u32[]{:S(2)}, u32[]{:S(2)}) %collective-permute-start.9) | collective-permute-done | bytes 294944 | tf_op jit(solution)/shard_map/ppermute | solution.py:448
  (149 shorter events, 94.9 us)
Async XLA Ops:
  7.2 90.4 %all-gather.5.cloned.1.call-start = ((), (), s32[]{:S(2)}) async-start(), calls=%async_computation | async-start | bytes 8515584 | tf_op jit(solution)/shard_map/all_gather | solution.py:529
  18.0 163.9 %all-gather.7.cloned.1.call-start = ((), (), s32[]{:S(2)}) async-start(), calls=%async_computation.1 | async-start | bytes 9732096 | tf_op jit(solution)/shard_map/all_gather | solution.py:530
  41.5 2.8 copy-start.10
  41.5 3.7 copy-start.8
  41.5 4.6 copy-start.12
  41.5 5.4 %copy-start.13 = (s32[3]{0:T(128)S(1)}, s32[3]{0:T(128)}, u32[]{:S(2)}) copy-start(s32[3]{0:T(128)} %constant.359.clone.1) | copy-start | bytes 40
  285.9 5.5 %copy-start.11 = (f32[8,768]{1,0:T(8,128)S(1)}, f32[8,768]{1,0:T(8,128)}, u32[]{:S(2)}) copy-start(f32[8,768]{1,0:T(8,128)} %get-tuple-element.132) | copy-start | bytes 73732
  285.9 5.7 %copy-start.9 = (f32[1,3072]{1,0:T(1,128)S(1)}, f32[1,3072]{1,0:T(1,128)}, u32[]{:S(2)}) copy-start(f32[1,3072]{1,0:T(1,128)} %get-tuple-element.133) | copy-start | bytes 36868
  285.9 9.6 %copy-start.6 = (bf16[768,768]{1,0:T(8,128)(2,1)S(1)}, bf16[768,768]{1,0:T(8,128)(2,1)}, u32[]{:S(2)}) copy-start(bf16[768,768]{1,0:T(8,128)(2,1)} %get-tuple-element.129) | copy-start | bytes 3538948
  291.7 12.5 %slice-start = ((s8[4718592]{0:T(1024)(128)(4,1)}), s8[524288]{0:T(1024)(128)(4,1)S(1)}, s32[]{:S(2)}) async-start(s8[4718592]{0:T(1024)(128)(4,1)} %bitcast.128), calls=%async_computation.2 | async-start | bytes 1048576
  295.5 8.8 %slice-start.1 = ((s8[4718592]{0:T(1024)(128)(4,1)}), s8[4194304]{0:T(1024)(128)(4,1)S(1)}, s32[]{:S(2)}) async-start(s8[4718592]{0:T(1024)(128)(4,1)} %bitcast.128), calls=%async_computation.3 | async-start | bytes 8388608
  299.7 4.5 copy-start
  302.2 7.4 %collective-permute-start = (bf16[8,2,168,768]{3,2,1,0:T(8,128)(2,1)}, bf16[8,2,168,768]{3,2,1,0:T(8,128)(2,1)}, u32[]{:S(2)}, u32[]{:S(2)}) collective-permute-start(bf16[8,2,168,768]{3,2,1,0:T(8,128)(2,1)} %dynamic-slice_bitcast_fusion), channel_id=1, source_target_pairs={{0,2},{1,3},{2,0},{3,1},{4,6},{5,7},{6,4},{7,5},{8,10},{9,11},{10,... | collective-permute-start | bytes 12386312 | tf_op jit(solution)/shard_map/ppermute | solution.py:448
  304.3 15.1 %slice-start.2 = ((s8[4718592]{0:T(1024)(128)(4,1)}), s8[524288]{0:T(1024)(128)(4,1)S(1)}, s32[]{:S(2)}) async-start(s8[4718592]{0:T(1024)(128)(4,1)} %bitcast.131), calls=%async_computation.4 | async-start | bytes 1048576
  308.6 10.8 %collective-permute-start.5 = (bf16[8,2,192,768]{3,2,1,0:T(8,128)(2,1)}, bf16[8,2,192,768]{3,2,1,0:T(8,128)(2,1)}, u32[]{:S(2)}, u32[]{:S(2)}) collective-permute-start(bf16[8,2,192,768]{3,2,1,0:T(8,128)(2,1)} %fusion.3), channel_id=1, source_target_pairs={{0,2},{1,3},{2,0},{3,1},{4,6},{5,7},{6,4},{7,5},{8,10},{9,11},{10,... | collective-permute-start | bytes 14155784 | tf_op jit(solution)/shard_map/ppermute | solution.py:448
  308.8 10.5 %slice-start.3 = ((s8[4718592]{0:T(1024)(128)(4,1)}), s8[4194304]{0:T(1024)(128)(4,1)S(1)}, s32[]{:S(2)}) async-start(s8[4718592]{0:T(1024)(128)(4,1)} %bitcast.131), calls=%async_computation.5 | async-start | bytes 8388608
  317.9 48.1 %collective-permute-start.1 = (bf16[8,1,168,768]{3,2,1,0:T(8,128)(2,1)}, bf16[8,1,168,768]{3,2,1,0:T(8,128)(2,1)}, u32[]{:S(2)}, u32[]{:S(2)}) collective-permute-start(bf16[8,1,168,768]{3,2,1,0:T(8,128)(2,1)} %constant_dynamic-slice_fusion.3), channel_id=1, source_target_pairs={{0,1},{1,0},{2,3},{3,2},{4,5},{5,4},{6,7},{7,6},{8,9},{9,8},{10,11... | collective-permute-start | bytes 6193160 | tf_op jit(solution)/shard_map/ppermute | solution.py:448
  327.9 87.9 %collective-permute-start.6 = (bf16[8,1,192,768]{3,2,1,0:T(8,128)(2,1)S(1)}, bf16[8,1,192,768]{3,2,1,0:T(8,128)(2,1)}, u32[]{:S(2)}, u32[]{:S(2)}) collective-permute-start(bf16[8,1,192,768]{3,2,1,0:T(8,128)(2,1)S(1)} %constant_dynamic-slice_fusion.1), channel_id=1, source_target_pairs={{0,1},{1,0},{2,3},{3,2},{4,5},{5,4},{6,7},{7,6},{8,9},{9,8},{10,11... | collective-permute-start | bytes 7077896 | tf_op jit(solution)/shard_map/ppermute | solution.py:448
  370.0 51.3 %collective-permute-start.2 = (bf16[4,1,168,768]{3,2,0,1:T(8,128)(2,1)S(1)}, bf16[4,1,168,768]{3,2,0,1:T(8,128)(2,1)}, u32[]{:S(2)}, u32[]{:S(2)}) collective-permute-start(bf16[4,1,168,768]{3,2,0,1:T(8,128)(2,1)S(1)} %dynamic-slice_bitcast_fusion.2), channel_id=1, source_target_pairs={{0,4},{1,5},{2,6},{3,7},{4,0},{5,1},{6,2},{7,3},{8,12},{9,13},{10,... | collective-permute-start | bytes 3096584 | tf_op jit(solution)/shard_map/ppermute | solution.py:448
  371.5 49.8 %copy-start.3 = (bf16[8,1,168,768]{3,2,1,0:T(8,128)(2,1)S(1)}, bf16[8,1,168,768]{3,2,1,0:T(8,128)(2,1)}, u32[]{:S(2)}) copy-start(bf16[8,1,168,768]{3,2,1,0:T(8,128)(2,1)} %copy-done.2) | copy-start | bytes 6193156
  419.9 51.5 %collective-permute-start.7 = (bf16[4,1,192,768]{3,2,0,1:T(8,128)(2,1)}, bf16[4,1,192,768]{3,2,0,1:T(8,128)(2,1)}, u32[]{:S(2)}, u32[]{:S(2)}) collective-permute-start(bf16[4,1,192,768]{3,2,0,1:T(8,128)(2,1)} %dynamic-slice_bitcast_fusion.1), channel_id=1, source_target_pairs={{0,4},{1,5},{2,6},{3,7},{4,0},{5,1},{6,2},{7,3},{8,12},{9,13},{10,... | collective-permute-start | bytes 3538952 | tf_op jit(solution)/shard_map/ppermute | solution.py:448
  423.6 43.9 %collective-permute-start.3 = (bf16[2,1,168,768]{3,2,0,1:T(8,128)(2,1)}, bf16[2,1,168,768]{3,2,0,1:T(8,128)(2,1)}, u32[]{:S(2)}, u32[]{:S(2)}) collective-permute-start(bf16[2,1,168,768]{3,2,0,1:T(8,128)(2,1)} %dynamic-slice_bitcast_fusion.4), channel_id=1, source_target_pairs={{0,8},{1,9},{2,10},{3,11},{4,12},{5,13},{6,14},{7,15},{8,0},{9,1},... | collective-permute-start | bytes 1548296 | tf_op jit(solution)/shard_map/ppermute | solution.py:448
  451.5 1.3 collective-permute-start.10
  452.8 4.6 collective-permute-start.11
  457.4 4.5 collective-permute-start.12
  461.9 4.5 collective-permute-start.13
  464.1 9.5 %copy-start.7 = (bf16[576,768]{1,0:T(8,128)(2,1)S(1)}, bf16[576,768]{1,0:T(8,128)(2,1)}, u32[]{:S(2)}) copy-start(bf16[576,768]{1,0:T(8,128)(2,1)} %get-tuple-element.119) | copy-start | bytes 2654212
  466.5 11.1 %collective-permute-start.14 = (f32[160,12]{1,0:T(8,128)S(1)}, f32[160,12]{1,0:T(8,128)S(1)}, u32[]{:S(2)}, u32[]{:S(2)}) collective-permute-start(f32[160,12]{1,0:T(8,128)S(1)} %add.192), channel_id=1, source_target_pairs={{0,16},{1,17},{2,18},{3,19},{4,20},{5,21},{6,22},{7,23},{8,24},{9,... | collective-permute-start | bytes 23048 | tf_op jit(solution)/shard_map/ppermute | solution.py:448
  469.5 13.4 %collective-permute-start.4 = (bf16[1,1,168,768]{3,2,0,1:T(8,128)(2,1)}, bf16[1,1,168,768]{3,2,0,1:T(8,128)(2,1)}, u32[]{:S(2)}, u32[]{:S(2)}) collective-permute-start(bf16[1,1,168,768]{3,2,0,1:T(8,128)(2,1)} %constant_dynamic-slice_fusion.2), channel_id=1, source_target_pairs={{0,16},{1,17},{2,18},{3,19},{4,20},{5,21},{6,22},{7,23},{8,24},{9,... | collective-permute-start | bytes 774152 | tf_op jit(solution)/shard_map/ppermute | solution.py:448
  473.0 9.9 %copy-start.5 = (bf16[2,1,168,768]{3,2,0,1:T(8,128)(2,1)S(1)}, bf16[2,1,168,768]{3,2,0,1:T(8,128)(2,1)}, u32[]{:S(2)}) copy-start(bf16[2,1,168,768]{3,2,0,1:T(8,128)(2,1)} %copy-done.4) | copy-start | bytes 1548292
  473.0 17.1 %collective-permute-start.8 = (bf16[2,1,192,768]{3,2,0,1:T(8,128)(2,1)S(1)}, bf16[2,1,192,768]{3,2,0,1:T(8,128)(2,1)S(1)}, u32[]{:S(2)}, u32[]{:S(2)}) collective-permute-start(bf16[2,1,192,768]{3,2,0,1:T(8,128)(2,1)S(1)} %dynamic-slice_bitcast_fusion.3), channel_id=1, source_target_pairs={{0,8},{1,9},{2,10},{3,11},{4,12},{5,13},{6,14},{7,15},{8,0},{9,1},... | collective-permute-start | bytes 1769480 | tf_op jit(solution)/shard_map/ppermute | solution.py:448
  490.3 12.4 %collective-permute-start.9 = (bf16[1,1,192,768]{3,2,0,1:T(8,128)(2,1)S(1)}, bf16[1,1,192,768]{3,2,0,1:T(8,128)(2,1)S(1)}, u32[]{:S(2)}, u32[]{:S(2)}) collective-permute-start(bf16[1,1,192,768]{3,2,0,1:T(8,128)(2,1)S(1)} %constant_dynamic-slice_fusion), channel_id=1, source_target_pairs={{0,16},{1,17},{2,18},{3,19},{4,20},{5,21},{6,22},{7,23},{8,24},{9,... | collective-permute-start | bytes 884744 | tf_op jit(solution)/shard_map/ppermute | solution.py:448
  (3 other events, 6.1 us)
Sparse Core Ops, SparseCore 0:
  18.1 79.4 all-gather.4
  101.1 80.7 all-gather.6
